TPU v7x, 512 devices: a whole 4x8x8 slice. The times are simulated.
512 devices in a mesh: grp: 8 (over y), row: 8 (over z), col: 8 (over x, core).
Axes of the slice: x: 4, y: 8, z: 8, core: 2. Of those that a mesh axis runs over, the one named last changes fastest.
Arguments:
- new_rows: bfloat16 [768, 16, 8192], P(('grp', 'col'), None, 'row'), may hold values from -6 to 6
- query_weight: bfloat16 [8192, 8192], P('row', 'col')
- key_weight: bfloat16 [8192, 1024], P('row', 'col')
- value_weight: bfloat16 [8192, 1024], P('row', 'col'), may hold values from -0.0625 to 0.0625
- cache_keys: bfloat16 [768, 512, 1024], P(('grp', 'row'), None, 'col'), may hold values from -6 to 6
- cache_values: bfloat16 [768, 512, 1024], P(('grp', 'row'), None, 'col'), may hold values from -6 to 6
- region_agents: int32 [768], replicated, may hold values from 0 to 767, as said below
- new_counts: int32 [768], replicated, may hold values from 4 to 16, as said below
- cache_lengths: int32 [768], replicated, may hold values from 1 to 512, as said below
Outputs:
- attended: bfloat16 [768, 16, 8192], P(('grp', 'col'), 'row')
Inputs may be any that keep to these rules, and one draw needn't show every extreme that they name: `region_agents`: A permutation of the 768 agents. Rows i with equal i // 12 form one region; agent a is served by group a // 96. Every region holds at most 3 agents served by one group, and exactly 3 of some group. `new_counts`: some agent has 16 new tokens. `cache_lengths`: some agent has 512 cached positions.
All inputs are finite; a program needn't handle non-finite values.
Results may differ from a plain program's by a relative error of at most 0.025.
Values may be sent and summed in bfloat16 or wider, within the bound.
A program may use at most 64 MiB of HBM per device.

v0:
```python
import jax
import jax.numpy as jnp
from jax import lax
from jax.sharding import PartitionSpec as P

HEAD_DIM = 128
rotary_base = 500000.0
floor_score = -1e30


def rotate_pairs(values, positions):
    half_dim = values.shape[-1] // 2
    exponent = jnp.arange(half_dim, dtype=jnp.float32) * (2.0 / values.shape[-1])
    frequency = rotary_base ** (-exponent)
    angles = positions.astype(jnp.float32)[..., None, None] * frequency
    cosine = jnp.cos(angles)
    sine_part = jnp.sin(angles)
    first_half = values[..., :half_dim]
    second = values[..., half_dim:]
    return jnp.concatenate(
        [first_half * cosine - second * sine_part, second * cosine + first_half * sine_part],
        axis=-1,
    )


def local(
    new_rows,
    query_weight,
    key_weight,
    value_weight,
    cache_keys,
    cache_values,
    region_agents,
    new_counts,
    cache_lengths,
):
    groups = lax.axis_size("grp")
    grid_rows = lax.axis_size("row")
    grid_cols = lax.axis_size("col")
    group_index = lax.axis_index("grp")
    row_index = lax.axis_index("row")
    col_index = lax.axis_index("col")
    agents_total = region_agents.shape[0]
    per_group = agents_total // groups
    per_region = new_rows.shape[0]
    regions = groups * grid_cols
    capacity = max(2, 2 * per_region // groups)
    slot_count = new_rows.shape[1]
    feature_width = new_rows.shape[2]
    slot_width = slot_count // grid_cols
    served_by = region_agents // per_group
    grouped = served_by.reshape(regions, per_region)
    earlier = jnp.arange(per_region)[:, None] > jnp.arange(per_region)[None, :]
    same_group = grouped[:, :, None] == grouped[:, None, :]
    bucket = jnp.sum((same_group & earlier[None, :, :]).astype(jnp.int32), axis=2).reshape(
        agents_total
    )
    slot_of_agent = jnp.argsort(region_agents)
    my_region = group_index * grid_cols + col_index
    mine_group = lax.dynamic_slice_in_dim(served_by, my_region * per_region, per_region)
    mine_bucket = lax.dynamic_slice_in_dim(bucket, my_region * per_region, per_region)
    choose = (
        (mine_group[None, None, :] == jnp.arange(groups)[:, None, None])
        & (mine_bucket[None, None, :] == jnp.arange(capacity)[None, :, None])
    ).astype(jnp.bfloat16)
    pieces = new_rows.reshape(per_region, grid_cols, slot_width, feature_width)
    outgoing = jnp.einsum(
        "gkj,jcsd->gcksd", choose, pieces, preferred_element_type=jnp.float32
    ).astype(jnp.bfloat16)
    arrived = lax.all_to_all(
        outgoing.reshape(regions, capacity, slot_width, feature_width),
        ("grp", "col"),
        split_axis=0,
        concat_axis=0,
        tiled=True,
    )
    my_slots = lax.dynamic_slice_in_dim(slot_of_agent, group_index * per_group, per_group)
    source_row = my_slots // per_region * capacity + jnp.take(bucket, my_slots)
    landed = jnp.take(
        arrived.reshape(regions * capacity, slot_width, feature_width), source_row, axis=0
    )
    tokens = lax.all_gather(landed, "col", axis=1, tiled=True)
    agents_here = cache_keys.shape[0]
    picked = tokens.reshape(lax.axis_size("row") * agents_here * slot_count, feature_width)
    query_part = jnp.dot(picked, query_weight, preferred_element_type=jnp.float32)
    key_part = jnp.dot(picked, key_weight, preferred_element_type=jnp.float32)
    value_part = jnp.dot(picked, value_weight, preferred_element_type=jnp.float32)
    summed = lax.psum_scatter(
        jnp.concatenate([query_part, key_part, value_part], axis=1)
        .reshape(lax.axis_size("row") * agents_here, slot_count, -1)
        .astype(jnp.bfloat16),
        "row",
        scatter_dimension=0,
        tiled=True,
    ).astype(jnp.float32)
    local_agents = (
        group_index * per_group + row_index * agents_here + jnp.arange(agents_here, dtype=jnp.int32)
    )
    lengths_now = jnp.take(cache_lengths, local_agents)
    counts_now = jnp.take(new_counts, local_agents)
    positions = lengths_now[:, None] + jnp.arange(slot_count, dtype=jnp.int32)[None, :]
    query_width = query_weight.shape[1]
    key_width = key_weight.shape[1]
    heads_here = query_width // HEAD_DIM
    kv_here = key_width // HEAD_DIM
    group_ratio = heads_here // kv_here
    queries = rotate_pairs(
        summed[:, :, :query_width].reshape(agents_here, slot_count, heads_here, HEAD_DIM), positions
    ).astype(jnp.bfloat16)
    fresh_keys = rotate_pairs(
        summed[:, :, query_width : query_width + key_width].reshape(
            agents_here, slot_count, kv_here, HEAD_DIM
        ),
        positions,
    ).astype(jnp.bfloat16)
    fresh_values = (
        summed[:, :, query_width + key_width :]
        .reshape(agents_here, slot_count, kv_here, HEAD_DIM)
        .astype(jnp.bfloat16)
    )
    query_rows = (
        queries.reshape(agents_here, slot_count, kv_here, group_ratio, HEAD_DIM)
        .transpose(0, 2, 3, 1, 4)
        .reshape(agents_here, kv_here, group_ratio * slot_count, HEAD_DIM)
    )
    cache_span = cache_keys.shape[1]
    stored_keys = cache_keys.reshape(agents_here, cache_span, kv_here, HEAD_DIM)
    stored_values = cache_values.reshape(agents_here, cache_span, kv_here, HEAD_DIM)
    score_scale = HEAD_DIM ** (-0.5)
    slot_of_row = jnp.arange(group_ratio * slot_count, dtype=jnp.int32) % slot_count
    fresh_index = jnp.arange(slot_count, dtype=jnp.int32)
    new_allowed = (
        (fresh_index[None, :] <= slot_of_row[:, None])[None, :, :]
        & (fresh_index[None, None, :] < counts_now[:, None, None])
    )[:, None, :, :]
    new_scores = (
        jnp.einsum("akrd,atkd->akrt", query_rows, fresh_keys, preferred_element_type=jnp.float32)
        * score_scale
    )
    cache_scores = (
        jnp.einsum("akrd,apkd->akrp", query_rows, stored_keys, preferred_element_type=jnp.float32)
        * score_scale
    )
    cache_allowed = (jnp.arange(cache_span, dtype=jnp.int32)[None, :] < lengths_now[:, None])[
        :, None, None, :
    ]
    cache_masked = jnp.where(cache_allowed, cache_scores, floor_score)
    new_masked = jnp.where(new_allowed, new_scores, floor_score)
    row_max = jnp.maximum(jnp.max(cache_masked, axis=3), jnp.max(new_masked, axis=3))
    cache_weights = jnp.where(cache_allowed, jnp.exp(cache_masked - row_max[..., None]), 0.0)
    new_weights = jnp.where(new_allowed, jnp.exp(new_masked - row_max[..., None]), 0.0)
    denominator = jnp.sum(cache_weights, axis=3) + jnp.sum(new_weights, axis=3)
    weighted = jnp.einsum(
        "akrp,apkd->akrd",
        cache_weights.astype(jnp.bfloat16),
        stored_values,
        preferred_element_type=jnp.float32,
    )
    weighted = weighted + jnp.einsum(
        "akrp,apkd->akrd",
        new_weights.astype(jnp.bfloat16),
        fresh_values,
        preferred_element_type=jnp.float32,
    )
    result = (
        (weighted / denominator[..., None])
        .reshape(agents_here, kv_here, group_ratio, slot_count, HEAD_DIM)
        .transpose(0, 3, 1, 2, 4)
        .reshape(agents_here, slot_count, query_width)
    )
    valid_slot = jnp.arange(slot_count, dtype=jnp.int32)[None, :] < counts_now[:, None]
    result = jnp.where(valid_slot[:, :, None], result, 0.0).astype(jnp.bfloat16)
    regrouped = lax.all_to_all(result, "row", split_axis=1, concat_axis=0, tiled=True)
    slot_share = slot_count // grid_rows
    choose_back = (
        jnp.arange(regions * capacity, dtype=jnp.int32)[:, None] == source_row[None, :]
    ).astype(jnp.bfloat16)
    returning = jnp.einsum(
        "qt,tsf->qsf", choose_back, regrouped, preferred_element_type=jnp.float32
    ).astype(jnp.bfloat16)
    incoming = lax.all_to_all(
        returning.reshape(regions, capacity, slot_share, query_width),
        ("grp", "col"),
        split_axis=0,
        concat_axis=0,
        tiled=True,
    ).reshape(groups, grid_cols, capacity, slot_share, query_width)
    select_back = (
        (mine_group[:, None, None] == jnp.arange(groups)[None, :, None])
        & (mine_bucket[:, None, None] == jnp.arange(capacity)[None, None, :])
    ).astype(jnp.bfloat16)
    finished = jnp.einsum(
        "jgk,gcksf->jscf", select_back, incoming, preferred_element_type=jnp.float32
    ).astype(jnp.bfloat16)
    return finished.reshape(per_region, slot_share, grid_cols * query_width)


def solution(mesh):
    placed = (
        P(("grp", "col"), None, "row"),
        P("row", "col"),
        P("row", "col"),
        P("row", "col"),
        P(("grp", "row"), None, "col"),
        P(("grp", "row"), None, "col"),
        P(),
        P(),
        P(),
    )
    return jax.shard_map(
        local, mesh=mesh, in_specs=placed, out_specs=P(("grp", "col"), "row", None), check_vma=False
    )
```

profile of v0, /device:TPU:1, one launch (start us, length us, event | category | flops | bytes accessed | tf_op | source)
XLA Modules:
  0.0 230.3 jit_solution(6798773412891268803)
XLA Ops:
  6.5 0.8 add_select_fusion
  7.4 0.1 eq.103
  7.5 0.1 copy.72
  7.6 0.1 convert_reduce_fusion
  7.7 0.1 copy.74
  7.8 0.1 reshape.407
  7.9 0.1 dynamic_slice.10
  8.0 0.1 dynamic_slice.11
  8.1 1.2 copy.95
  9.3 0.3 fusion.11
  9.7 0.4 copy.122
  10.1 1.7 copy.77
  11.8 11.6 %all-to-all-start = ((bf16[64,3,2,1024]{3,2,1,0:T(2,128)(2,1)}), bf16[64,3,2,1024]{3,2,1,0:T(2,128)(2,1)S(1)}, u32[]{:S(2)}, u32[]{:S(2)}) async-start(bf16[64,3,2,1024]{3,2,1,0:T(2,128)(2,1)} %copy.77), calls=%async_computation | async-start | bytes 1572864 | tf_op jit(solution)/shard_map/all_to_all | solution.py:70
  23.5 4.4 %sort.17 = (s32[768]{0:T(1024)}, s32[768]{0:T(1024)S(1)}) sort(s32[768]{0:T(1024)S(1)} %copy-done.7, s32[768]{0:T(1024)S(1)} %iota.103), dimensions={0}, to_apply=%region_0.1 | sort | flops 7680 | bytes 12288 | tf_op jit(solution)/shard_map/jit(argsort)/sort | solution.py:58
  27.9 0.1 compare_select_fusion.2
  27.9 1.0 gather_fusion
  28.9 0.1 compare_and_fusion.1
  29.0 17.1 %all-to-all-done = bf16[64,3,2,1024]{3,2,1,0:T(2,128)(2,1)S(1)} async-done(((bf16[64,3,2,1024]{3,2,1,0:T(2,128)(2,1)}), bf16[64,3,2,1024]{3,2,1,0:T(2,128)(2,1)S(1)}, u32[]{:S(2)}, u32[]{:S(2)}) %all-to-all-start) | async-done | bytes 786464 | tf_op jit(solution)/shard_map/all_to_all | solution.py:70
  46.2 1.4 gather_fusion.1
  47.5 0.5 broadcast_select_fusion
  48.0 0.8 copy.78
  48.8 0.2 reduce-scatter.2.cloned.1.call-start
  49.1 33.5 %all-gather.2.cloned.1.call-done = bf16[96,16,1024]{2,0,1:T(8,128)(2,1)} async-done(((bf16[96,2,1024]{2,0,1:T(8,128)(2,1)}), bf16[96,16,1024]{2,0,1:T(8,128)(2,1)}) %all-gather.2.cloned.1.call-update) | async-done | bytes 3145744 | tf_op jit(solution)/shard_map/all_gather | solution.py:82
  82.6 3.6 %copy.79 = bf16[96,16,1024]{2,1,0:T(8,128)(2,1)S(1)} copy(bf16[96,16,1024]{2,0,1:T(8,128)(2,1)} %all-gather.2.cloned.1.call-done) | data formatting | bytes 6291456 | tf_op jit(solution)/shard_map/all_gather | solution.py:82
  86.2 3.8 %convolution_convert_fusion = bf16[1536,1024]{0,1:T(8,128)(2,1)S(1)} fusion(bf16[1536,1024]{1,0:T(8,128)(2,1)S(1)} %bitcast.78, bf16[1024,1024]{1,0:T(8,128)(2,1)S(1)} %copy-done), kind=kOutput, calls=%fused_computation.5 | convolution fusion | flops 3222798336 | bytes 8388608 | tf_op jit(solution)/shard_map/dot_general | solution.py:85
  90.1 1.2 convolution_convert_fusion.1
  91.3 1.2 convolution_convert_fusion.2
  92.5 2.1 pad_maximum_fusion
  94.5 6.3 %copy.80 = bf16[1536,1280]{1,0:T(8,128)(2,1)} copy(bf16[1536,1280]{0,1:T(8,128)(2,1)} %pad_maximum_fusion) | data formatting | bytes 7864320 | tf_op jit(solution)/shard_map/concatenate | solution.py:89
  100.9 0.6 copy-done.1
  101.5 0.6 gather_fusion.2
  102.1 0.6 gather_fusion.3
  102.8 0.1 iota_compare_fusion.3
  102.9 0.1 add_convert_fusion.1
  103.0 0.1 iota_compare_fusion.1
  103.0 0.4 multiply_cosine_fusion.1
  103.5 53.5 %reduce-scatter.2.cloned.1.call-done = bf16[12,16,1280]{2,1,0:T(8,128)(2,1)} async-done(((bf16[96,16,1280]{2,1,0:T(8,128)(2,1)}), bf16[12,16,1280]{2,1,0:T(8,128)(2,1)}) %reduce-scatter.2.cloned.1.call-update) | async-done | bytes 491536 | tf_op jit(solution)/shard_map/reduce_scatter | solution.py:88
  157.0 1.1 slice.37
  158.1 0.1 copy.102
  158.3 0.3 fusion.59
  158.6 0.1 convert_element_type.65
  158.7 0.5 fusion.40
  159.1 0.4 fusion.16
  159.5 0.2 pad_maximum_fusion.1
  159.7 0.2 copy-done.4
  160.0 0.7 fusion
  160.7 0.4 fusion.60
  161.0 0.1 fusion.29
  161.1 1.0 fusion.1
  162.2 1.1 fusion.3
  163.2 0.7 fusion.12
  163.9 0.1 copy.121
  164.0 0.2 reshape.416
  164.2 0.1 select_convert_fusion
  164.3 0.2 copy.84
  164.6 19.7 %all_to_all.28 = bf16[12,16,1024]{2,0,1:T(8,128)(2,1)S(1)} all-to-all(bf16[12,16,1024]{2,0,1:T(8,128)(2,1)S(1)} %copy.84), channel_id=1, replica_groups=mesh['grp'=8,'row'=8,'col'=8] {'row'}, dimensions={1} | all-to-all | bytes 786432 | tf_op jit(solution)/shard_map/all_to_all | solution.py:173
  184.3 0.4 copy.97
  184.7 0.4 convolution_convert_fusion.3
  185.1 1.7 copy.88
  186.7 12.2 %all-to-all-start.2 = ((bf16[64,3,2,1024]{3,2,1,0:T(2,128)(2,1)}), bf16[64,3,2,1024]{3,2,1,0:T(2,128)(2,1)S(1)}, u32[]{:S(2)}, u32[]{:S(2)}) async-start(bf16[64,3,2,1024]{3,2,1,0:T(2,128)(2,1)} %bitcast.24), calls=%async_computation.3 | async-start | bytes 1572864 | tf_op jit(solution)/shard_map/all_to_all | solution.py:181
  199.0 22.7 %all-to-all-done.2 = bf16[64,3,2,1024]{3,2,1,0:T(2,128)(2,1)S(1)} async-done(((bf16[64,3,2,1024]{3,2,1,0:T(2,128)(2,1)}), bf16[64,3,2,1024]{3,2,1,0:T(2,128)(2,1)S(1)}, u32[]{:S(2)}, u32[]{:S(2)}) %all-to-all-start.2) | async-done | bytes 786464 | tf_op jit(solution)/shard_map/all_to_all | solution.py:181
  221.7 0.6 fusion.13
  222.2 0.2 copy.91
  222.5 1.0 reshape.419
  (37 shorter events, 0.2 us)
Async XLA Ops:
  6.5 79.7 %copy-start = (bf16[1024,1024]{1,0:T(8,128)(2,1)S(1)}, bf16[1024,1024]{1,0:T(8,128)(2,1)}, u32[]{:S(2)}) copy-start(bf16[1024,1024]{1,0:T(8,128)(2,1)} %param.12) | copy-start | bytes 6291460
  9.3 14.2 %copy-start.7 = (s32[768]{0:T(1024)S(1)}, s32[768]{0:T(1024)}, u32[]{:S(2)}) copy-start(s32[768]{0:T(1024)} %param.17) | copy-start | bytes 9220
  11.8 34.4 %all-to-all-start = ((bf16[64,3,2,1024]{3,2,1,0:T(2,128)(2,1)}), bf16[64,3,2,1024]{3,2,1,0:T(2,128)(2,1)S(1)}, u32[]{:S(2)}, u32[]{:S(2)}) async-start(bf16[64,3,2,1024]{3,2,1,0:T(2,128)(2,1)} %copy.77), calls=%async_computation | async-start | bytes 1572864 | tf_op jit(solution)/shard_map/all_to_all | solution.py:70
  23.4 59.2 %all-gather.2.cloned.1.call-start = ((), (), s32[]{:S(2)}) async-start(), calls=%async_computation.4 | async-start | bytes 3538944 | tf_op jit(solution)/shard_map/all_gather | solution.py:82
  48.8 108.1 %reduce-scatter.2.cloned.1.call-start = ((), (), s32[]{:S(2)}) async-start(), calls=%async_computation.5 | async-start | bytes 4423680 | tf_op jit(solution)/shard_map/reduce_scatter | solution.py:88
  86.2 3.8 %copy-start.5 = (bf16[1024,128]{1,0:T(8,128)(2,1)S(1)}, bf16[1024,128]{1,0:T(8,128)(2,1)}, u32[]{:S(2)}) copy-start(bf16[1024,128]{1,0:T(8,128)(2,1)} %param.14) | copy-start | bytes 786436
  90.1 1.2 copy-start.6
  100.8 0.7 copy-start.1
  100.8 1.3 copy-start.2
  157.0 1.6 copy-start.3
  158.5 1.4 copy-start.4
  160.6 1.5 copy-start.8
  186.7 34.9 %all-to-all-start.2 = ((bf16[64,3,2,1024]{3,2,1,0:T(2,128)(2,1)}), bf16[64,3,2,1024]{3,2,1,0:T(2,128)(2,1)S(1)}, u32[]{:S(2)}, u32[]{:S(2)}) async-start(bf16[64,3,2,1024]{3,2,1,0:T(2,128)(2,1)} %bitcast.24), calls=%async_computation.3 | async-start | bytes 1572864 | tf_op jit(solution)/shard_map/all_to_all | solution.py:181
Sparse Core Ops, SparseCore 0:
  49.0 33.5 all-gather.1
  100.9 55.9 reduce-scatter.1
where the time goes:
time: 231 us; the launch traced here: 230 us
  waiting for transfers between devices  127 us (55%)
  local copies, waits for them, and re-layouts  24.5 us (11%)
  starting transfers between devices  24.1 us (10%)
  blocking collectives  19.7 us (9%)
  between operations  13.8 us (6%)
  other arithmetic  11.2 us (5%)
  matrix products  10.2 us (4%)
    reduce_scatter x1, waiting for transfers between devices, local(): lax.psum_scatter(jnp.concatenate([query_part, key_part, value_part], axis...  53.5 us
    all_gather x1, waiting for transfers between devices, local(): tokens = lax.all_gather(landed, 'col', axis=1, tiled=True)  33.5 us
    all_to_all x1, waiting for transfers between devices, local(): lax.all_to_all(returning.reshape(regions, capacity, slot_share, query_wid...  22.7 us
    all_to_all x1, blocking collectives, local(): lax.all_to_all(result, 'row', split_axis=1, concat_axis=0, tiled=True)  19.7 us
    all_to_all x1, waiting for transfers between devices, local(): lax.all_to_all(outgoing.reshape(regions, capacity, slot_width, feature_wi...  17.1 us
    all_to_all x1, starting transfers between devices, local(): lax.all_to_all(returning.reshape(regions, capacity, slot_share, query_wid...  12.2 us
    all_to_all x1, starting transfers between devices, local(): lax.all_to_all(outgoing.reshape(regions, capacity, slot_width, feature_wi...  11.6 us
    concatenate x1, local copies, waits for them, and re-layouts, local(): jnp.concatenate([query_part, key_part, value_part], axis=1)  6.26 us
  transfers between devices with their start and end apart: 4, of which 4 were waited for; matrix products, arithmetic and copies ran while one was open for 3% of the time, Pallas kernels for 0%

commit v1 on v0

--- a/solution.py
+++ b/solution.py
@@ -170,7 +170,10 @@
     )
     valid_slot = jnp.arange(slot_count, dtype=jnp.int32)[None, :] < counts_now[:, None]
     result = jnp.where(valid_slot[:, :, None], result, 0.0).astype(jnp.bfloat16)
-    regrouped = lax.all_to_all(result, "row", split_axis=1, concat_axis=0, tiled=True)
+    regrouped = jnp.concatenate(
+        lax.all_to_all(jnp.stack(jnp.split(result, lax.axis_size("row"), axis=1)), "row", 0, 0),
+        axis=0,
+    )
     slot_share = slot_count // grid_rows
     choose_back = (
         jnp.arange(regions * capacity, dtype=jnp.int32)[:, None] == source_row[None, :]

time: 231 us -> 228 us (0.987)
  blocking collectives: 19.7 us -> 17.2 us
    all_to_all x1, blocking collectives: 19.7 us -> 17.2 us  [local(): lax.all_to_all(jnp.stack(jnp.split(result, lax.axis_size('row'), axis=1))...]
where the time goes in v1:
time: 228 us; the launch traced here: 227 us
  waiting for transfers between devices  127 us (56%)
  local copies, waits for them, and re-layouts  24.3 us (11%)
  starting transfers between devices  23.7 us (10%)
  blocking collectives  17.2 us (8%)
  between operations  13.9 us (6%)
  other arithmetic  11.2 us (5%)
  matrix products  10.2 us (4%)
    reduce_scatter x1, waiting for transfers between devices, local(): lax.psum_scatter(jnp.concatenate([query_part, key_part, value_part], axis...  53.5 us
    all_gather x1, waiting for transfers between devices, local(): tokens = lax.all_gather(landed, 'col', axis=1, tiled=True)  33.5 us
    all_to_all x1, waiting for transfers between devices, local(): lax.all_to_all(returning.reshape(regions, capacity, slot_share, query_wid...  22.7 us
    all_to_all x1, blocking collectives, local(): lax.all_to_all(jnp.stack(jnp.split(result, lax.axis_size('row'), axis=1))...  17.2 us
    all_to_all x1, waiting for transfers between devices, local(): lax.all_to_all(outgoing.reshape(regions, capacity, slot_width, feature_wi...  17.1 us
    all_to_all x1, starting transfers between devices, local(): lax.all_to_all(returning.reshape(regions, capacity, slot_share, query_wid...  11.8 us
    all_to_all x1, starting transfers between devices, local(): lax.all_to_all(outgoing.reshape(regions, capacity, slot_width, feature_wi...  11.6 us
    concatenate x1, local copies, waits for them, and re-layouts, local(): jnp.concatenate([query_part, key_part, value_part], axis=1)  6.26 us
  transfers between devices with their start and end apart: 4, of which 4 were waited for; matrix products, arithmetic and copies ran while one was open for 3% of the time, Pallas kernels for 0%

profile of v1, /device:TPU:1, one launch (start us, length us, event | category | flops | bytes accessed | tf_op | source)
XLA Modules:
  0.0 227.4 jit_solution(4361786990367807276)
XLA Ops:
  6.5 0.8 add_select_fusion
  7.4 0.1 eq.103
  7.5 0.1 copy.72
  7.6 0.1 convert_reduce_fusion
  7.7 0.1 copy.74
  7.8 0.1 reshape.410
  7.9 0.1 dynamic_slice.10
  8.0 0.1 dynamic_slice.11
  8.1 1.2 copy.92
  9.3 0.3 fusion.11
  9.7 0.4 copy.117
  10.1 1.7 copy.77
  11.8 11.6 %all-to-all-start = ((bf16[64,3,2,1024]{3,2,1,0:T(2,128)(2,1)}), bf16[64,3,2,1024]{3,2,1,0:T(2,128)(2,1)S(1)}, u32[]{:S(2)}, u32[]{:S(2)}) async-start(bf16[64,3,2,1024]{3,2,1,0:T(2,128)(2,1)} %copy.77), calls=%async_computation | async-start | bytes 1572864 | tf_op jit(solution)/shard_map/all_to_all | solution.py:70
  23.5 4.4 %sort.17 = (s32[768]{0:T(1024)}, s32[768]{0:T(1024)S(1)}) sort(s32[768]{0:T(1024)S(1)} %copy-done.7, s32[768]{0:T(1024)S(1)} %iota.103), dimensions={0}, to_apply=%region_0.1 | sort | flops 7680 | bytes 12288 | tf_op jit(solution)/shard_map/jit(argsort)/sort | solution.py:58
  27.9 0.1 compare_select_fusion.2
  27.9 1.0 gather_fusion
  28.9 0.1 compare_and_fusion.1
  29.0 17.1 %all-to-all-done = bf16[64,3,2,1024]{3,2,1,0:T(2,128)(2,1)S(1)} async-done(((bf16[64,3,2,1024]{3,2,1,0:T(2,128)(2,1)}), bf16[64,3,2,1024]{3,2,1,0:T(2,128)(2,1)S(1)}, u32[]{:S(2)}, u32[]{:S(2)}) %all-to-all-start) | async-done | bytes 786464 | tf_op jit(solution)/shard_map/all_to_all | solution.py:70
  46.2 1.4 gather_fusion.1
  47.5 0.5 broadcast_select_fusion
  48.0 0.8 copy.78
  48.8 0.2 reduce-scatter.2.cloned.1.call-start
  49.1 33.5 %all-gather.2.cloned.1.call-done = bf16[96,16,1024]{2,0,1:T(8,128)(2,1)} async-done(((bf16[96,2,1024]{2,0,1:T(8,128)(2,1)}), bf16[96,16,1024]{2,0,1:T(8,128)(2,1)}) %all-gather.2.cloned.1.call-update) | async-done | bytes 3145744 | tf_op jit(solution)/shard_map/all_gather | solution.py:82
  82.6 3.6 %copy.79 = bf16[96,16,1024]{2,1,0:T(8,128)(2,1)S(1)} copy(bf16[96,16,1024]{2,0,1:T(8,128)(2,1)} %all-gather.2.cloned.1.call-done) | data formatting | bytes 6291456 | tf_op jit(solution)/shard_map/all_gather | solution.py:82
  86.2 3.8 %convolution_convert_fusion = bf16[1536,1024]{0,1:T(8,128)(2,1)S(1)} fusion(bf16[1536,1024]{1,0:T(8,128)(2,1)S(1)} %bitcast.106, bf16[1024,1024]{1,0:T(8,128)(2,1)S(1)} %copy-done), kind=kOutput, calls=%fused_computation.5 | convolution fusion | flops 3222798336 | bytes 8388608 | tf_op jit(solution)/shard_map/dot_general | solution.py:85
  90.1 1.2 convolution_convert_fusion.1
  91.3 1.2 convolution_convert_fusion.2
  92.5 2.1 pad_maximum_fusion
  94.5 6.3 %copy.80 = bf16[1536,1280]{1,0:T(8,128)(2,1)} copy(bf16[1536,1280]{0,1:T(8,128)(2,1)} %pad_maximum_fusion) | data formatting | bytes 7864320 | tf_op jit(solution)/shard_map/concatenate | solution.py:89
  100.9 0.6 copy-done.1
  101.5 0.6 gather_fusion.2
  102.1 0.6 gather_fusion.3
  102.8 0.1 iota_compare_fusion.3
  102.9 0.1 add_convert_fusion.1
  103.0 0.1 iota_compare_fusion.1
  103.0 0.4 multiply_cosine_fusion.1
  103.5 53.5 %reduce-scatter.2.cloned.1.call-done = bf16[12,16,1280]{2,1,0:T(8,128)(2,1)} async-done(((bf16[96,16,1280]{2,1,0:T(8,128)(2,1)}), bf16[12,16,1280]{2,1,0:T(8,128)(2,1)}) %reduce-scatter.2.cloned.1.call-update) | async-done | bytes 491536 | tf_op jit(solution)/shard_map/reduce_scatter | solution.py:88
  157.0 1.1 slice.37
  158.1 0.1 copy.97
  158.3 0.3 fusion.67
  158.6 0.1 convert_element_type.65
  158.7 0.5 fusion.48
  159.1 0.4 fusion.16
  159.5 0.2 pad_maximum_fusion.1
  159.7 0.2 copy-done.4
  160.0 0.7 fusion
  160.7 0.4 fusion.68
  161.0 0.1 fusion.29
  161.1 1.0 fusion.1
  162.2 1.1 fusion.3
  163.2 0.7 fusion.12
  163.9 0.1 copy.116
  164.0 0.2 reshape.419
  164.2 0.1 select_convert_fusion
  164.4 0.1 fusion.38
  164.5 0.1 fusion.37
  164.8 17.2 %all_to_all.15 = bf16[8,12,2,1024]{3,2,1,0:T(2,128)(2,1)S(1)} all-to-all(bf16[8,12,2,1024]{3,2,1,0:T(2,128)(2,1)S(1)} %fusion.32), channel_id=1, replica_groups=mesh['grp'=8,'row'=8,'col'=8] {'row'}, dimensions={0} | all-to-all | bytes 786432 | tf_op jit(solution)/shard_map/all_to_all | solution.py:174
  182.0 0.4 convolution_convert_fusion.3
  182.4 1.7 copy.85
  184.1 11.8 %all-to-all-start.2 = ((bf16[64,3,2,1024]{3,2,1,0:T(2,128)(2,1)}), bf16[64,3,2,1024]{3,2,1,0:T(2,128)(2,1)S(1)}, u32[]{:S(2)}, u32[]{:S(2)}) async-start(bf16[64,3,2,1024]{3,2,1,0:T(2,128)(2,1)} %bitcast.29), calls=%async_computation.3 | async-start | bytes 1572864 | tf_op jit(solution)/shard_map/all_to_all | solution.py:184
  196.0 22.7 %all-to-all-done.2 = bf16[64,3,2,1024]{3,2,1,0:T(2,128)(2,1)S(1)} async-done(((bf16[64,3,2,1024]{3,2,1,0:T(2,128)(2,1)}), bf16[64,3,2,1024]{3,2,1,0:T(2,128)(2,1)S(1)}, u32[]{:S(2)}, u32[]{:S(2)}) %all-to-all-start.2) | async-done | bytes 786464 | tf_op jit(solution)/shard_map/all_to_all | solution.py:184
  218.7 0.6 fusion.13
  219.3 0.2 copy.88
  219.5 1.0 reshape.423
  (43 shorter events, 0.5 us)
Async XLA Ops:
  6.5 79.7 %copy-start = (bf16[1024,1024]{1,0:T(8,128)(2,1)S(1)}, bf16[1024,1024]{1,0:T(8,128)(2,1)}, u32[]{:S(2)}) copy-start(bf16[1024,1024]{1,0:T(8,128)(2,1)} %param.12) | copy-start | bytes 6291460
  9.3 14.2 %copy-start.7 = (s32[768]{0:T(1024)S(1)}, s32[768]{0:T(1024)}, u32[]{:S(2)}) copy-start(s32[768]{0:T(1024)} %param.17) | copy-start | bytes 9220
  11.8 34.4 %all-to-all-start = ((bf16[64,3,2,1024]{3,2,1,0:T(2,128)(2,1)}), bf16[64,3,2,1024]{3,2,1,0:T(2,128)(2,1)S(1)}, u32[]{:S(2)}, u32[]{:S(2)}) async-start(bf16[64,3,2,1024]{3,2,1,0:T(2,128)(2,1)} %copy.77), calls=%async_computation | async-start | bytes 1572864 | tf_op jit(solution)/shard_map/all_to_all | solution.py:70
  23.4 59.2 %all-gather.2.cloned.1.call-start = ((), (), s32[]{:S(2)}) async-start(), calls=%async_computation.4 | async-start | bytes 3538944 | tf_op jit(solution)/shard_map/all_gather | solution.py:82
  48.8 108.1 %reduce-scatter.2.cloned.1.call-start = ((), (), s32[]{:S(2)}) async-start(), calls=%async_computation.5 | async-start | bytes 4423680 | tf_op jit(solution)/shard_map/reduce_scatter | solution.py:88
  86.2 3.8 %copy-start.5 = (bf16[1024,128]{1,0:T(8,128)(2,1)S(1)}, bf16[1024,128]{1,0:T(8,128)(2,1)}, u32[]{:S(2)}) copy-start(bf16[1024,128]{1,0:T(8,128)(2,1)} %param.14) | copy-start | bytes 786436
  90.1 1.2 copy-start.6
  100.8 0.7 copy-start.1
  100.8 1.3 copy-start.2
  157.0 1.6 copy-start.3
  158.5 1.4 copy-start.4
  160.6 1.5 copy-start.8
  184.1 34.6 %all-to-all-start.2 = ((bf16[64,3,2,1024]{3,2,1,0:T(2,128)(2,1)}), bf16[64,3,2,1024]{3,2,1,0:T(2,128)(2,1)S(1)}, u32[]{:S(2)}, u32[]{:S(2)}) async-start(bf16[64,3,2,1024]{3,2,1,0:T(2,128)(2,1)} %bitcast.29), calls=%async_computation.3 | async-start | bytes 1572864 | tf_op jit(solution)/shard_map/all_to_all | solution.py:184
Sparse Core Ops, SparseCore 0:
  49.0 33.5 all-gather.1
  100.9 55.9 reduce-scatter.1
